TPU v7x, 256 devices: a whole 4x4x8 slice. The times are simulated.
256 devices in a mesh: dp: 8 (over z), expert: 32 (over x, y, core).
Axes of the slice: x: 4, y: 4, z: 8, core: 2. Of those that a mesh axis runs over, the one named last changes fastest.
Arguments:
- tokens: bfloat16 [12288, 2048], P(('dp', 'expert')), may hold values from -6 to 6
- tokens_dot: bfloat16 [12288, 2048], P(('dp', 'expert')), may hold values from -6 to 6
- router: bfloat16 [2048, 64], replicated, may hold values from -0.125 to 0.125
- router_dot: bfloat16 [2048, 64], replicated, may hold values from -0.125 to 0.125
- expert_ids: int32 [12288, 8], P(('dp', 'expert')), may hold values from 0 to 63, all different within a row; in each aligned block of 48 rows (0 to 47, 48 to 95, ...) at most 12 rows name the same one
- priority: int32 [12288], P(('dp', 'expert')), may hold values from 0 to 12287, each once
- w_gate: bfloat16 [64, 768, 2048], P('expert', 'dp'), may hold values from -0.125 to 0.125
- w_up: bfloat16 [64, 768, 2048], P('expert', 'dp'), may hold values from -0.125 to 0.125
- w_down: bfloat16 [64, 768, 2048], P('expert', 'dp'), may hold values from -0.21875 to 0.21875
Outputs:
- mixed: bfloat16 [12288, 2048], P(('dp', 'expert'))
- mixed_dot: bfloat16 [12288, 2048], P(('dp', 'expert'))
Inputs may be any that keep to these rules, and one draw needn't show every extreme that they name: `expert_ids`: each token names 8 different experts; among the tokens of one device no expert is named more than 12 times, and exactly 12 times in some device. `priority`: each rank appears once.
All inputs are finite; a program needn't handle non-finite values.
Results may differ from a plain program's by a relative error of at most 0.0058.
Values may be sent and summed in bfloat16 or wider, within the bound.
A program may use at most 128 MiB of HBM per device.

v0:
```python
import jax
import jax.numpy as jnp
from jax import lax
from jax.sharding import PartitionSpec as P

TOP = 8
MOST = 12
CAP = 192


def hidden_units(stacked, gate_piece, up_piece):
    gate_all = jnp.einsum("ercd,efd->ercf", stacked, gate_piece, preferred_element_type=jnp.float32)
    up_all = jnp.einsum("ercd,efd->ercf", stacked, up_piece, preferred_element_type=jnp.float32)
    gate_p = gate_all[:, 0]
    up_p = up_all[:, 0]
    sigma = 1.0 / (1.0 + jnp.exp(-gate_p))
    act = gate_p * sigma * up_p
    act_dot = (
        sigma * (1.0 + gate_p * (1.0 - sigma)) * gate_all[:, 1] * up_p
        + gate_p * sigma * up_all[:, 1]
    )
    return jnp.stack([act, act_dot], axis=1).astype(jnp.bfloat16)


def shards(tokens, tokens_dot, router, router_dot, expert_ids, priority, w_gate, w_up, w_down):
    tok_count = tokens.shape[0]
    feat_width = tokens.shape[1]
    expert_count = router.shape[1]
    local_count = w_gate.shape[0]
    peer_count = lax.axis_size("expert")
    slot_count = MOST
    sentinel = 2**30
    member = (
        expert_ids[:, :, None] == jnp.arange(expert_count, dtype=jnp.int32)[None, None, :]
    ).astype(jnp.int32)
    member_flat = member.reshape(tok_count * TOP, expert_count)
    before = jnp.cumsum(member_flat, axis=0) - member_flat
    slot_index = jnp.sum(before * member_flat, axis=1)
    target = expert_ids.reshape(-1) * slot_count + slot_index
    owner_tok = jnp.arange(tok_count * TOP, dtype=jnp.int32) // TOP
    joined = jnp.concatenate([tokens, tokens_dot], axis=1)
    outgoing = (
        jnp.zeros((expert_count * slot_count, 2 * feat_width), jnp.bfloat16)
        .at[target]
        .set(joined[owner_tok])
    )
    out_ranks = (
        jnp.full((expert_count * slot_count,), sentinel, jnp.int32)
        .at[target]
        .set(priority[owner_tok])
    )
    outgoing = outgoing.reshape(peer_count, local_count * slot_count, 2 * feat_width)
    out_ranks = out_ranks.reshape(peer_count, local_count * slot_count)
    arrived, arrived_rank = (
        lax.all_to_all(outgoing, "expert", split_axis=0, concat_axis=0, tiled=True),
        lax.all_to_all(out_ranks, "expert", split_axis=0, concat_axis=0, tiled=True),
    )
    arrived = arrived.reshape(peer_count, local_count, slot_count, 2, feat_width)
    rank_local = jnp.transpose(
        arrived_rank.reshape(peer_count, local_count, slot_count), (1, 0, 2)
    ).reshape(local_count, peer_count * slot_count)
    usable = rank_local < sentinel
    ahead = jnp.sum(
        (usable[:, None, :] & (rank_local[:, None, :] < rank_local[:, :, None])).astype(jnp.int32),
        axis=2,
    )
    kept = usable & (ahead < CAP)
    placing = (
        kept[:, None, :] & (ahead[:, None, :] == jnp.arange(CAP, dtype=jnp.int32)[None, :, None])
    ).astype(jnp.bfloat16)
    placing = placing.reshape(local_count, CAP, peer_count, slot_count)
    packed = jnp.einsum(
        "ecsm,semrd->ercd", placing, arrived, preferred_element_type=jnp.float32
    ).astype(jnp.bfloat16)
    gate_piece = lax.all_gather(w_gate, "dp", axis=1, tiled=True)
    up_piece = lax.all_gather(w_up, "dp", axis=1, tiled=True)
    down_piece = lax.all_gather(w_down, "dp", axis=1, tiled=True)
    hidden = hidden_units(packed, gate_piece, up_piece)
    expert_out = jnp.einsum(
        "ercf,efd->ercd", hidden, down_piece, preferred_element_type=jnp.float32
    )
    out_bf = expert_out.astype(jnp.bfloat16)
    returning = jnp.einsum(
        "ecsm,ercd->semrd", placing, out_bf, preferred_element_type=jnp.float32
    ).astype(jnp.bfloat16)
    returning = returning.reshape(peer_count, local_count * slot_count, 2 * feat_width)
    landed = lax.all_to_all(returning, "expert", split_axis=0, concat_axis=0, tiled=True)
    landed = landed.reshape(expert_count * slot_count, 2, feat_width)
    results = landed[target].reshape(tok_count, TOP, 2, feat_width).astype(jnp.float32)
    logits = jnp.dot(tokens, router, preferred_element_type=jnp.float32)
    logits_dot = jnp.dot(tokens_dot, router, preferred_element_type=jnp.float32) + jnp.dot(
        tokens, router_dot, preferred_element_type=jnp.float32
    )
    member_f = member.astype(jnp.float32)
    chosen = jnp.sum(member_f * logits[:, None, :], axis=2)
    chosen_dot = jnp.sum(member_f * logits_dot[:, None, :], axis=2)
    expo = jnp.exp(chosen)
    gates = expo / jnp.sum(expo, axis=1, keepdims=True)
    gates_dot = gates * (chosen_dot - jnp.sum(gates * chosen_dot, axis=1, keepdims=True))
    mixed = jnp.sum(gates[:, :, None] * results[:, :, 0], axis=1)
    mixed_dot = jnp.sum(
        gates_dot[:, :, None] * results[:, :, 0] + gates[:, :, None] * results[:, :, 1], axis=1
    )
    return (mixed.astype(jnp.bfloat16), mixed_dot.astype(jnp.bfloat16))


def solution(mesh):
    return jax.shard_map(
        shards,
        mesh=mesh,
        in_specs=(
            P(("dp", "expert"), None),
            P(("dp", "expert"), None),
            P(),
            P(),
            P(("dp", "expert"), None),
            P(("dp", "expert")),
            P("expert", "dp", None),
            P("expert", "dp", None),
            P("expert", "dp", None),
        ),
        out_specs=(P(("dp", "expert"), None), P(("dp", "expert"), None)),
        check_vma=False,
    )
```

profile of v0, /device:TPU:8, one launch (start us, length us, event | category | flops | bytes accessed | tf_op | source)
XLA Modules:
  0.0 415.2 jit_solution(13426487562719504342)
XLA Ops:
  7.2 0.7 all-gather.4.cloned.1.call-update
  8.0 0.7 all-gather.6.cloned.1.call-update
  8.7 0.7 all-gather.8.cloned.1.call-update
  9.4 0.8 copy.37
  10.4 0.9 reduce-window.6
  11.6 0.7 broadcast_multiply_fusion
  12.6 1.7 fusion.48
  14.3 2.1 fusion.46
  16.4 2.1 fusion.47
  18.5 30.2 %select_select_fusion = s32[384]{0:T(512)S(1)} fusion(s32[384]{0:T(512)S(1)} %fusion.43, s32[]{:T(128)} %bitcast.2, s32[]{:T(128)} %bitcast.3, s32[]{:T(128)} %bitcast.4, s32[]{:T(128)} %bitcast.5, s32[]{:T(128)} %bitcast.6, s32[]{:T(128)} %bitcast.7, s32[]{:T(128)} %bitcast.8, s32[]{:T(128)} %bitcast.9, s32[]{:T(128)} %bitcast.10, s32[]{:T(128)} %bitcast.11, ...), kind=kLoop, calls=%fused_computation.72 | loop fusion | flops 36096 | bytes 3264 | tf_op jit(solution)/shard_map/gather | solution.py:50
  48.7 2.9 scatter_custom_fusion.1
  51.6 0.7 all_to_all.13
  52.3 8.2 %all-to-all-start.1 = ((s32[32,1,24]{2,1,0:T(1,128)}), s32[32,1,24]{2,1,0:T(1,128)S(1)}, u32[]{:S(2)}, u32[]{:S(2)}) async-start(s32[32,1,24]{2,1,0:T(1,128)} %bitcast.50), calls=%async_computation.1 | async-start | bytes 32768 | tf_op jit(solution)/shard_map/all_to_all | solution.py:56
  60.5 17.9 %scatter_custom_fusion = bf16[768,4096]{1,0:T(8,128)(2,1)} fusion(s32[384]{0:T(512)S(1)} %fusion.42, bf16[48,4096]{1,0:T(8,128)(2,1)S(1)} %pad_maximum_fusion, s32[1024]{0:T(1024)S(1)} %pad_clamp_fusion.1, bf16[]{:T(256)} %constant.15.clone.1), kind=kCustom, calls=%fused_computation.22 | custom fusion | bytes 6291458 | tf_op jit(solution)/shard_map/scatter | solution.py:45
  78.4 7.4 %all-to-all-start = ((bf16[32,24,4096]{2,1,0:T(8,128)(2,1)}), bf16[32,24,4096]{2,1,0:T(8,128)(2,1)}, u32[]{:S(2)}, u32[]{:S(2)}) async-start(bf16[32,24,4096]{2,1,0:T(8,128)(2,1)} %bitcast.133), calls=%async_computation | async-start | bytes 12582912 | tf_op jit(solution)/shard_map/all_to_all | solution.py:55
  86.7 86.7 %all-to-all-done = bf16[32,24,4096]{2,1,0:T(8,128)(2,1)} async-done(((bf16[32,24,4096]{2,1,0:T(8,128)(2,1)}), bf16[32,24,4096]{2,1,0:T(8,128)(2,1)}, u32[]{:S(2)}, u32[]{:S(2)}) %all-to-all-start) | async-done | bytes 6291488 | tf_op jit(solution)/shard_map/all_to_all | solution.py:55
  173.4 11.5 %reshape.196 = bf16[32,2,12,2,2048]{4,3,2,1,0:T(2,128)(2,1)} reshape(bf16[32,24,4096]{2,1,0:T(8,128)(2,1)} %all-to-all-done) | data formatting | bytes 12582912 | tf_op jit(solution)/shard_map/reshape | solution.py:58
  184.9 8.9 %bitcast_convert_fusion = bf16[2,2,2048,192]{2,3,1,0:T(8,128)(2,1)} fusion(bf16[32,2,12,2,2048]{4,3,2,1,0:T(2,128)(2,1)} %reshape.196, s32[2,32,12]{1,2,0:T(8,128)S(1)} %copy.45, pred[2,32,12]{1,2,0:T(8,128)(4,1)S(1)} %compare_and_fusion), kind=kOutput, calls=%fused_computation.10 | convolution fusion | flops 1209827328 | bytes 9441024 | tf_op jit(solution)/shard_map/ecsm,semrd->ercd/dot_general | solution.py:72
  193.8 6.4 %fusion.4 = f32[2,2,192,768]{3,2,1,0:T(8,128)S(1)} fusion(bf16[2,768,2048]{2,1,0:T(8,128)(2,1)} %all-gather.4.cloned.1.call-done, bf16[2,2,2048,192]{2,3,1,0:T(8,128)(2,1)} %bitcast_convert_fusion), kind=kOutput, calls=%fused_computation.8 | convolution fusion | flops 2415919104 | bytes 11796480 | tf_op jit(solution)/shard_map/ercd,efd->ercf/dot_general | solution.py:12
  200.3 6.4 %fusion.2 = f32[2,2,192,768]{3,2,1,0:T(8,128)S(1)} fusion(bf16[2,768,2048]{2,1,0:T(8,128)(2,1)} %all-gather.6.cloned.1.call-done, bf16[2,2,2048,192]{2,3,1,0:T(8,128)(2,1)} %bitcast_convert_fusion), kind=kOutput, calls=%fused_computation.6 | convolution fusion | flops 2415919104 | bytes 11796480 | tf_op jit(solution)/shard_map/ercd,efd->ercf/dot_general | solution.py:13
  206.7 1.7 multiply_convert_fusion
  208.4 28.7 %all-gather.8.cloned.1.call-done = bf16[2,768,2048]{2,1,0:T(8,128)(2,1)} async-done(((bf16[2,96,2048]{2,1,0:T(8,128)(2,1)}), bf16[2,768,2048]{2,1,0:T(8,128)(2,1)}) %all-gather.8.cloned.1.call-update) | async-done | bytes 6291472 | tf_op jit(solution)/shard_map/all_gather | solution.py:77
  237.1 5.8 %fusion.10 = bf16[2,2,192,2048]{3,2,1,0:T(8,128)(2,1)S(1)} fusion(bf16[2,768,2048]{2,1,0:T(8,128)(2,1)} %all-gather.8.cloned.1.call-done, bf16[2,1,192,768]{3,2,1,0:T(8,128)(2,1)} %get-tuple-element.9, bf16[2,1,192,768]{3,2,1,0:T(8,128)(2,1)} %get-tuple-element.8), kind=kOutput, calls=%fused_computation.14 | convolution fusion | flops 2418081792 | bytes 10616832 | tf_op jit(solution)/shard_map/ercf,efd->ercd/dot_general | solution.py:79
  242.8 2.5 convert_bitcast_fusion
  245.4 14.0 %copy.48 = bf16[32,2,12,2,2048]{4,3,2,1,0:T(2,128)(2,1)} copy(bf16[32,2,12,2,2048]{4,0,2,3,1:T(8,128)(2,1)S(1)} %convert_bitcast_fusion) | data formatting | bytes 12582912 | tf_op jit(solution)/shard_map/convert_element_type | solution.py:85
  259.4 11.1 %reshape.199 = bf16[32,24,4096]{2,1,0:T(8,128)(2,1)} reshape(bf16[32,2,12,2,2048]{4,3,2,1,0:T(2,128)(2,1)} %copy.48) | data formatting | bytes 12582912 | tf_op jit(solution)/shard_map/reshape | solution.py:86
  270.5 7.6 %all-to-all-start.2 = ((bf16[32,24,4096]{2,1,0:T(8,128)(2,1)}), bf16[32,24,4096]{2,1,0:T(8,128)(2,1)}, u32[]{:S(2)}, u32[]{:S(2)}) async-start(bf16[32,24,4096]{2,1,0:T(8,128)(2,1)} %reshape.199), calls=%async_computation.2 | async-start | bytes 12582912 | tf_op jit(solution)/shard_map/all_to_all | solution.py:87
  279.4 86.3 %all-to-all-done.2 = bf16[32,24,4096]{2,1,0:T(8,128)(2,1)} async-done(((bf16[32,24,4096]{2,1,0:T(8,128)(2,1)}), bf16[32,24,4096]{2,1,0:T(8,128)(2,1)}, u32[]{:S(2)}, u32[]{:S(2)}) %all-to-all-start.2) | async-done | bytes 6291488 | tf_op jit(solution)/shard_map/all_to_all | solution.py:87
  365.6 11.1 %reshape.200 = bf16[768,2,2048]{2,1,0:T(2,128)(2,1)} reshape(bf16[32,24,4096]{2,1,0:T(8,128)(2,1)} %all-to-all-done.2) | data formatting | bytes 12582912 | tf_op jit(solution)/shard_map/reshape | solution.py:88
  376.8 17.7 %gather_fusion = bf16[384,2,2048]{2,1,0:T(2,128)(2,1)S(1)} fusion(bf16[768,2,2048]{2,1,0:T(2,128)(2,1)} %reshape.200, s32[1024]{0:T(1024)S(1)} %pad_clamp_fusion), kind=kCustom, calls=%fused_computation.1 | custom fusion | bytes 6292992 | tf_op jit(solution)/shard_map/gather | solution.py:89
  394.5 6.5 %fusion.45 = (f32[48,8,1,2048]{3,2,1,0:T(1,128)S(1)}, f32[48,8,1,2048]{3,2,1,0:T(1,128)}) fusion(bf16[48,8,2,2048]{3,2,1,0:T(2,128)(2,1)S(1)} %bitcast.132), kind=kLoop, calls=%fused_computation.80 | loop fusion | bytes 12582912 | tf_op jit(solution)/shard_map/slice | solution.py:100
  401.0 7.5 %fusion.14 = (bf16[48,2048]{1,0:T(8,128)(2,1)}, bf16[48,2048]{1,0:T(8,128)(2,1)}) fusion(f32[48,8,1,2048]{3,2,1,0:T(1,128)} %get-tuple-element.11, f32[48,8,1,2048]{3,2,1,0:T(1,128)S(1)} %get-tuple-element.10, f32[48,8]{1,0:T(8,128)S(1)} %subtract_multiply_fusion, f32[48,8]{1,0:T(8,128)S(1)} %get-tuple-element.7), kind=kLoop, calls=%fused_computation.18 | loop fusion | flops 4521984 | bytes 6687744 | tf_op jit(solution)/shard_map/reduce_sum | solution.py:101
  (43 shorter events, 3.1 us)
Async XLA Ops:
  7.2 270.9 %copy-start = (bf16[2048,64]{0,1:T(8,128)(2,1)S(1)}, bf16[2048,64]{0,1:T(8,128)(2,1)}, u32[]{:S(2)}) copy-start(bf16[2048,64]{0,1:T(8,128)(2,1)} %param.11) | copy-start | bytes 786436
  7.2 53.3 %copy-start.2 = (bf16[48,2048]{1,0:T(8,128)(2,1)S(1)}, bf16[48,2048]{1,0:T(8,128)(2,1)}, u32[]{:S(2)}) copy-start(bf16[48,2048]{1,0:T(8,128)(2,1)} %param.10) | copy-start | bytes 589828
  7.2 53.3 %copy-start.1 = (bf16[48,2048]{1,0:T(8,128)(2,1)S(1)}, bf16[48,2048]{1,0:T(8,128)(2,1)}, u32[]{:S(2)}) copy-start(bf16[48,2048]{1,0:T(8,128)(2,1)} %param.9) | copy-start | bytes 589828
  7.2 186.6 %all-gather.4.cloned.1.call-start = ((), (), s32[]{:S(2)}) async-start(), calls=%async_computation.3 | async-start | bytes 7077888 | tf_op jit(solution)/shard_map/all_gather | solution.py:75
  7.9 192.3 %all-gather.6.cloned.1.call-start = ((), (), s32[]{:S(2)}) async-start(), calls=%async_computation.4 | async-start | bytes 7077888 | tf_op jit(solution)/shard_map/all_gather | solution.py:76
  8.7 228.4 %all-gather.8.cloned.1.call-start = ((), (), s32[]{:S(2)}) async-start(), calls=%async_computation.5 | async-start | bytes 7077888 | tf_op jit(solution)/shard_map/all_gather | solution.py:77
  52.3 26.1 %all-to-all-start.1 = ((s32[32,1,24]{2,1,0:T(1,128)}), s32[32,1,24]{2,1,0:T(1,128)S(1)}, u32[]{:S(2)}, u32[]{:S(2)}) async-start(s32[32,1,24]{2,1,0:T(1,128)} %bitcast.50), calls=%async_computation.1 | async-start | bytes 32768 | tf_op jit(solution)/shard_map/all_to_all | solution.py:56
  78.4 95.0 %all-to-all-start = ((bf16[32,24,4096]{2,1,0:T(8,128)(2,1)}), bf16[32,24,4096]{2,1,0:T(8,128)(2,1)}, u32[]{:S(2)}, u32[]{:S(2)}) async-start(bf16[32,24,4096]{2,1,0:T(8,128)(2,1)} %bitcast.133), calls=%async_computation | async-start | bytes 12582912 | tf_op jit(solution)/shard_map/all_to_all | solution.py:55
  270.5 8.0 %copy-start.3 = (bf16[2048,64]{0,1:T(8,128)(2,1)S(1)}, bf16[2048,64]{0,1:T(8,128)(2,1)}, u32[]{:S(2)}) copy-start(bf16[2048,64]{0,1:T(8,128)(2,1)} %param.12) | copy-start | bytes 786436
  270.5 95.2 %all-to-all-start.2 = ((bf16[32,24,4096]{2,1,0:T(8,128)(2,1)}), bf16[32,24,4096]{2,1,0:T(8,128)(2,1)}, u32[]{:S(2)}, u32[]{:S(2)}) async-start(bf16[32,24,4096]{2,1,0:T(8,128)(2,1)} %reshape.199), calls=%async_computation.2 | async-start | bytes 12582912 | tf_op jit(solution)/shard_map/all_to_all | solution.py:87
Sparse Core Ops, SparseCore 0:
  9.8 77.3 all-gather.3
  89.0 73.0 all-gather.5
  163.9 73.0 all-gather.7
where the time goes:
time: 420 us; the launch traced here: 415 us
  waiting for transfers between devices  204 us (49%)
  local copies, waits for them, and re-layouts  101 us (24%)
  other arithmetic  42.2 us (10%)
  matrix products  30.7 us (7%)
  starting transfers between devices  23.3 us (6%)
  between operations  14.2 us (3%)
    all_to_all x1, waiting for transfers between devices, shards(): lax.all_to_all(outgoing, 'expert', split_axis=0, concat_axis=0, tiled=True)  86.7 us
    all_to_all x1, waiting for transfers between devices, shards(): lax.all_to_all(returning, 'expert', split_axis=0, concat_axis=0, tiled=True)  86.3 us
    gather x1, other arithmetic, shards(): priority[owner_tok]  30.2 us
    all_gather x1, waiting for transfers between devices, shards(): down_piece = lax.all_gather(w_down, 'dp', axis=1, tiled=True)  28.7 us
    scatter x1, local copies, waits for them, and re-layouts, shards(): outgoing = jnp.zeros((expert_count * slot_count, 2 * feat_width), jnp.bfl...  17.9 us
    gather x1, local copies, waits for them, and re-layouts, shards(): landed[target].reshape(tok_count, TOP, 2, feat_width).astype(jnp.float32)  17.7 us
    convert_element_type x1, local copies, waits for them, and re-layouts, shards(): returning = jnp.einsum('ecsm,ercd->semrd', placing, out_bf, preferred_ele...  14 us
    reshape x1, local copies, waits for them, and re-layouts, shards(): arrived.reshape(peer_count, local_count, slot_count, 2, feat_width)  11.5 us
  transfers between devices with their start and end apart: 6, of which 3 were waited for; matrix products, arithmetic and copies ran while one was open for 23% of the time, Pallas kernels for 0%

commit v1 on v0

v1 whole, which is shorter than its diff:
```python
import functools

import jax
import jax.numpy as jnp
from jax import lax
from jax.experimental import pallas as pl
from jax.experimental.pallas import tpu as pltpu
from jax.sharding import PartitionSpec as P

GRID = (4, 4, 2)
CAP = 192
PARTS = 4
LANES = 64
VMEM_BYTES = 66_500_000
F32 = jnp.float32
BF16 = jnp.bfloat16


def ring_order(pieces, hops, cost, latency):
    ready = {(p, 1): 0.0 for p in range(pieces)}
    clock, order, done = 0.0, [], {}
    while ready:
        there = sorted(k for k, t in ready.items() if t <= clock)
        if not there:
            clock = min(ready.values())
            continue
        p, h = there[0]
        del ready[(p, h)]
        order.append((clock, p, h))
        clock += cost[p] * (0.5 if h == hops else 1.0)
        if h < hops:
            ready[(p, h + 1)] = clock + latency
        else:
            done[p] = clock + latency
    return order, done


def body(nz, tok, tokd, rout, routd, ids, rank, wg, wu, wd, out, outd,
         g_all, u_all, d_all, t_all, m_all, x_all, hid, place, place_t, slot_g, yy, keep, xsum, rows,
         c_in, y_in2, y_in1, x_in2, x_in1,
         zs, zr, ts, tr, ms, mr, cs, cr, ys, yr, xs, xr, loc):
    nx, ny, nc = GRID
    me = lax.axis_index("expert")
    z = lax.axis_index("dp")
    c = lax.rem(me, nc)
    y = lax.rem(lax.div(me, nc), ny)
    x = lax.div(me, nc * ny)
    td, width = tok.shape
    units = wg.shape[1]
    ff = units * nz
    dq = width // PARTS
    qw = 2 * dq
    top = ids.shape[1]
    hops = nz // 2

    def dev(zz, xx, yc, cc):
        return {"dp": zz, "expert": (xx * ny + yc) * nc + cc}

    def step(v, by, n):
        return lax.rem(v + (by + n), n)

    z_nb = [dev(step(z, s, nz), x, y, c) for s in (1, -1)]
    x_nb = [dev(z, step(x, s, nx), y, c) for s in (1, -1)]
    y_nb = [dev(z, x, step(y, s, ny), c) for s in (1, -1)]
    sib = dev(z, x, y, 1 - c)

    partners = [sib] + (z_nb if nz > 1 else []) + (x_nb if nx > 1 else []) + (y_nb if ny > 1 else [])
    barrier = pltpu.get_barrier_semaphore()
    for p in partners:
        pl.semaphore_signal(barrier, inc=1, device_id=p, device_id_type=pl.DeviceIdType.MESH)
    pl.semaphore_wait(barrier, len(partners))

    sent = []

    def send(src, dst, ssem, rsem, device):
        copy = pltpu.make_async_remote_copy(
            src_ref=src, dst_ref=dst, send_sem=ssem, recv_sem=rsem,
            device_id=device, device_id_type=pl.DeviceIdType.MESH)
        copy.start()
        return copy

    def arrived(dst, ssem, rsem, device):
        pltpu.make_async_remote_copy(
            src_ref=dst, dst_ref=dst, send_sem=ssem, recv_sem=rsem,
            device_id=device, device_id_type=pl.DeviceIdType.MESH).wait_recv()

    half_units = units // 2

    def piece_own(p):
        if p < 4:
            return (wg, wu)[p % 2].at[p // 2]
        return wd.at[:, :, pl.ds((p - 4) * dq, dq)]

    def piece_view(p, zz):
        at = pl.ds(pl.multiple_of(zz * units, units), units)
        if p < 4:
            return (g_all, u_all)[p % 2].at[p // 2, at]
        return d_all.at[p - 4, :, at]

    def piece_half(p, zz, d):
        if p < 4:
            at = pl.ds(pl.multiple_of(zz * units + d * half_units, half_units), half_units)
            return (g_all, u_all)[p % 2].at[p // 2, at]
        return d_all.at[p - 4, d, pl.ds(pl.multiple_of(zz * units, units), units)]

    pieces = 4 + PARTS

    def own_copy(p):
        return pltpu.make_async_copy(piece_own(p), piece_view(p, z), loc.at[p])

    def z_send(p, h):
        for d in range(2):
            sign = (-1, 1)[d]
            if h == 1:
                src, dst = piece_own(p), piece_view(p, z)
            else:
                origin = step(z, sign * (h - 1), nz)
                arrived(piece_view(p, origin), zs.at[p, d, h - 2], zr.at[p, d, h - 2], z_nb[d])
                src = piece_view(p, origin) if h < hops else piece_half(p, origin, d)
                dst = src
            sent.append(send(src, dst, zs.at[p, d, h - 1], zr.at[p, d, h - 1], z_nb[d]))

    def z_done(p):
        own_copy(p).wait()
        if nz > 1:
            for d in range(2):
                origin = step(z, (-1, 1)[d] * hops, nz)
                arrived(piece_half(p, origin, d), zs.at[p, d, hops - 1], zr.at[p, d, hops - 1], z_nb[d])

    def gather_steps(buf, ssem, rsem, log):
        wide = buf.shape[-1] // 2

        def x_view(i):
            return buf.at[y, c, i]

        def x_half(i, d):
            return buf.at[y, c, i, :, pl.ds(d * wide, wide)]

        def y_view(i):
            return buf.at[i, c]

        def y_half(i, d):
            return buf.at[i, c, :, :, pl.ds(d * wide, wide)]

        def one(base, view, pos, nb):
            for d in range(2):
                log.append(send(view(pos), view(pos), ssem.at[base + d], rsem.at[base + d], nb[d]))

        def two(base, view, half, pos, n, nb):
            for d in range(2):
                origin = step(pos, (-1, 1)[d], n)
                arrived(view(origin), ssem.at[base + d], rsem.at[base + d], nb[d])
                log.append(send(half(origin, d), half(origin, d), ssem.at[base + 2 + d], rsem.at[base + 2 + d], nb[d]))

        def three(base, half, pos, n, nb):
            for d in range(2):
                origin = step(pos, (-2, 2)[d], n)
                arrived(half(origin, d), ssem.at[base + 2 + d], rsem.at[base + 2 + d], nb[d])

        def cross(k):
            i = step(y, (0, -1, 1, 2)[k], ny)
            log.append(send(buf.at[i, c], buf.at[i, c], ssem.at[8 + k], rsem.at[8 + k], sib))

        def x1():
            if nx > 1:
                one(0, x_view, x, x_nb)

        def x2():
            if nx > 1:
                two(0, x_view, x_half, x, nx, x_nb)

        def y1():
            if nx > 1:
                three(0, x_half, x, nx, x_nb)
            if ny > 1:
                one(4, y_view, y, y_nb)
            cross(0)

        def y2():
            if ny > 1:
                two(4, y_view, y_half, y, ny, y_nb)
                cross(1)
                cross(2)

        def y3():
            if ny > 1:
                three(4, y_half, y, ny, y_nb)
                cross(3)

        def end():
            for k in range(4 if ny > 1 else 1):
                i = step(y, (0, -1, 1, 2)[k], ny)
                arrived(buf.at[i, 1 - c], ssem.at[8 + k], rsem.at[8 + k], sib)

        return x1, x2, y1, y2, y3, end

    t_log, m_log = [], []
    t_steps = gather_steps(t_all, ts, tr, t_log)
    m_steps = gather_steps(m_all, ms, mr, m_log)

    def tokens_start():
        t_all[y, c, x, :, pl.ds(0, width)] = tok[...]
        t_all[y, c, x, :, pl.ds(width, width)] = tokd[...]
        t_steps[0]()

    def routing_start():
        logits = jnp.dot(tok[...], rout[...], preferred_element_type=F32)
        logits_dot = jnp.dot(tokd[...], rout[...], preferred_element_type=F32) + jnp.dot(
            tok[...], routd[...], preferred_element_type=F32)
        lane = lax.broadcasted_iota(jnp.int32, (td, LANES), 1)
        member = jnp.zeros((td, LANES), F32)
        for k in range(top):
            member = jnp.where(lane == ids[:, k:k + 1], 1.0, member)
        chosen = member > 0.5
        expo = jnp.where(chosen, jnp.exp(jnp.where(chosen, logits, 0.0)), 0.0)
        gates = expo / jnp.sum(expo, axis=1, keepdims=True)
        sel_dot = jnp.where(chosen, logits_dot, 0.0)
        gates_dot = jnp.where(chosen, gates * (sel_dot - jnp.sum(gates * sel_dot, axis=1, keepdims=True)), 0.0)
        own_rank = jnp.broadcast_to(rank[...].astype(F32), (td, LANES))
        m_all[y, c, x] = jnp.concatenate([gates, gates_dot, member, own_rank], axis=1)
        m_steps[0]()

    group = nc * nx * td
    slots = 2 * CAP

    def routing_rows():
        lane = lax.broadcasted_iota(jnp.int32, (group, 4 * LANES), 1)
        lane_s = lax.broadcasted_iota(jnp.int32, (group, 128), 1)

        @pl.loop(0, ny)
        def _(i):
            m = m_all[i].reshape(group, 4 * LANES)
            picked = jnp.zeros((group, 128), F32)
            columns = [3 * LANES] + [2 * LANES + 2 * me + e for e in range(2)]
            columns += [2 * me + e for e in range(2)] + [LANES + 2 * me + e for e in range(2)]
            for j, col in enumerate(columns):
                v = jnp.sum(jnp.where(lane == col, m, 0.0), axis=1, keepdims=True)
                picked = jnp.where(lane_s == j, v, picked)
            rows[i] = jnp.transpose(picked)[0:8]

    def routing_ahead():
        whole = jnp.concatenate([rows[i] for i in range(ny)], axis=1)
        rank_t = whole[0:1]
        ahead = jnp.zeros((8, ny * group), F32)
        for i in range(ny):
            rank_s = m_all[i].reshape(group, 4 * LANES)[:, 3 * LANES:3 * LANES + 1]
            lower = jnp.where(rank_s < rank_t, 1.0, 0.0).astype(BF16)
            ahead = ahead + jnp.dot(rows[i].astype(BF16), lower, preferred_element_type=F32)
        seat = lax.broadcasted_iota(jnp.int32, (CAP, ny * group), 0).astype(F32)
        for e in range(2):
            here = jnp.where(whole[1 + e:2 + e] > 0.5, ahead[1 + e:2 + e], -1.0)
            hit = here == seat
            place[pl.ds(e * CAP, CAP)] = jnp.where(hit, 1.0, 0.0).astype(BF16)
            for r in range(2):
                slot_g[r, e] = jnp.sum(jnp.where(hit, whole[3 + 2 * r + e:4 + 2 * r + e], 0.0), axis=1, keepdims=True)

    def routing_turn():
        for i in range(ny):
            block = place[:, pl.ds(i * group, group)].astype(F32)
            place_t[i] = jnp.transpose(block).astype(BF16).reshape(nc, nx * td, slots)

    col = min(256, width)

    def pack(r, lo, hi):
        @pl.loop(lo, hi)
        def _(n):
            at = pl.multiple_of(n * col, col)
            picked = t_all[:, :, :, :, pl.ds(pl.multiple_of(r * width + at, col), col)].reshape(ny * group, col)
            res = jnp.dot(place[...], picked, preferred_element_type=F32).astype(BF16)
            for e in range(2):
                x_all[e, r, :, pl.ds(at, col)] = res[e * CAP:(e + 1) * CAP]

    fcol = 256 if ff % 256 == 0 else ff
    nt = (((1,), (1,)), ((), ()))

    def hidden(e, n):
        at = pl.ds(n * fcol, fcol)
        both = x_all[e].reshape(slots, width)
        ga = lax.dot_general(both, g_all[e, at], nt, preferred_element_type=F32)
        ua = lax.dot_general(both, u_all[e, at], nt, preferred_element_type=F32)
        gp, gt, up, ut = ga[:CAP], ga[CAP:], ua[:CAP], ua[CAP:]
        sigma = 1.0 / (1.0 + jnp.exp(-gp))
        hid[e, 0, :, at] = (gp * sigma * up).astype(BF16)
        hid[e, 1, :, at] = (sigma * (1.0 + gp * (1.0 - sigma)) * gt * up + gp * sigma * ut).astype(BF16)

    back_log = []

    def down(q):
        for e in range(2):
            res = jnp.dot(hid[e].reshape(slots, ff), d_all[q, e], preferred_element_type=F32)
            prim, tang = res[:CAP], res[CAP:]
            g, gd = slot_g[0, e], slot_g[1, e]
            yy[pl.ds(e * CAP, CAP), pl.ds(0, dq)] = (g * prim).astype(BF16)
            yy[pl.ds(e * CAP, CAP), pl.ds(dq, dq)] = (gd * prim + g * tang).astype(BF16)

    y_turn = (2, 1, -1, 0) if ny > 1 else (0,)

    def give(q):
        cols = pl.ds(q * qw, qw)
        for k, by in enumerate(y_turn):
            i = step(y, by, ny)
            res = jnp.dot(place_t[i, 1 - c], yy[...], preferred_element_type=F32)
            t_all[i, 0, :, :, cols] = res.astype(BF16).reshape(nx, td, qw)
            back_log.append(send(t_all.at[i, 0, :, :, cols], c_in.at[q, i], cs.at[q, k], cr.at[q, k], sib))
        for by in y_turn:
            i = step(y, by, ny)
            res = jnp.dot(place_t[i, c], yy[...], preferred_element_type=F32)
            keep[q % 2, i] = res.reshape(nx, td, qw)

    def summed(q, by):
        i = step(y, by, ny)
        k = y_turn.index(by)
        arrived(c_in.at[q, i], cs.at[q, k], cr.at[q, k], sib)
        return keep[q % 2, i] + c_in[q, i].astype(F32)

    lo, hi = pl.ds(0, dq), pl.ds(dq, dq)

    def y_first(q):
        if ny == 1:
            return
        cols = q * qw
        t_all[0, 1, :, :, pl.ds(cols, qw)] = summed(q, 2).astype(BF16)
        for d in range(2):
            src = t_all.at[0, 1, :, :, pl.ds(cols + d * dq, dq)]
            back_log.append(send(src, y_in2.at[q, :, :, pl.ds(d * dq, dq)], ys.at[q, d], yr.at[q, d], y_nb[d]))

    def y_second(q):
        if ny == 1:
            return
        cols = q * qw
        for d in range(2):
            v = summed(q, (1, -1)[d])
            mine = t_all.at[1 + d, 1, :, :, pl.ds(cols, qw)]
            got = y_in2.at[q, :, :, pl.ds(d * dq, dq)]
            arrived(got, ys.at[q, d], yr.at[q, d], y_nb[d])
            a, b = v[:, :, :dq], v[:, :, dq:]
            if d == 0:
                a = a + got[...].astype(F32)
            else:
                b = b + got[...].astype(F32)
            t_all[1 + d, 1, :, :, pl.ds(cols, dq)] = a.astype(BF16)
            t_all[1 + d, 1, :, :, pl.ds(cols + dq, dq)] = b.astype(BF16)
            back_log.append(send(mine, y_in1.at[q, d], ys.at[q, 2 + d], yr.at[q, 2 + d], y_nb[d]))

    def y_third(q):
        v = summed(q, 0)
        if ny > 1:
            for d in range(2):
                arrived(y_in1.at[q, d], ys.at[q, 2 + d], yr.at[q, 2 + d], y_nb[d])
                v = v + y_in1[q, d].astype(F32)
        xsum[q % 2] = v
        if nx > 1:
            cols = q * qw
            t_all[ny - 1, 1, 0, :, pl.ds(cols, qw)] = xsum[q % 2, step(x, 2, nx)].astype(BF16)
            for d in range(2):
                src = t_all.at[ny - 1, 1, 0, :, pl.ds(cols + d * dq, dq)]
                back_log.append(send(src, x_in2.at[q, :, pl.ds(d * dq, dq)], xs.at[q, d], xr.at[q, d], x_nb[d]))

    def x_second(q):
        if nx == 1:
            return
        cols = q * qw
        for d in range(2):
            v = xsum[q % 2, step(x, (1, -1)[d], nx)]
            got = x_in2.at[q, :, pl.ds(d * dq, dq)]
            arrived(got, xs.at[q, d], xr.at[q, d], x_nb[d])
            a, b = v[:, :dq], v[:, dq:]
            if d == 0:
                a = a + got[...].astype(F32)
            else:
                b = b + got[...].astype(F32)
            t_all[ny - 1, 1, 1 + d, :, pl.ds(cols, dq)] = a.astype(BF16)
            t_all[ny - 1, 1, 1 + d, :, pl.ds(cols + dq, dq)] = b.astype(BF16)
            src = t_all.at[ny - 1, 1, 1 + d, :, pl.ds(cols, qw)]
            back_log.append(send(src, x_in1.at[q, d], xs.at[q, 2 + d], xr.at[q, 2 + d], x_nb[d]))

    def x_third(q):
        v = xsum[q % 2, x]
        if nx > 1:
            for d in range(2):
                arrived(x_in1.at[q, d], xs.at[q, 2 + d], xr.at[q, 2 + d], x_nb[d])
                v = v + x_in1[q, d].astype(F32)
        out[:, pl.ds(q * dq, dq)] = v[:, :dq].astype(BF16)
        outd[:, pl.ds(q * dq, dq)] = v[:, dq:].astype(BF16)

    def settle_tokens():
        for copy in t_log + m_log:
            copy.wait_send()

    plan = []

    def at(t, f, *a):
        plan.append((t, len(plan), f, a))

    tau = 9.0
    cost = [tau] * 4 + [2 * tau / PARTS] * PARTS
    if nz > 1:
        order, done = ring_order(pieces, hops, cost, 2.0)
    else:
        order, done = [], {p: 60.0 + 15.0 * p for p in range(pieces)}
    started = sum(1 for t, p, h in order if h == 1 and t <= tau)
    for t, p, h in order:
        at(-1.0 if h == 1 and t <= tau else t - 0.9 * tau / 2 if h == 1 else t - 0.1, z_send, p, h)
    for p in range(pieces):
        at(-0.5, lambda p: own_copy(p).start(), p)
    at(0.0, routing_start)
    at(0.5, tokens_start)
    at(5.0, m_steps[1])
    at(12.0, m_steps[2])
    at(13.0, t_steps[1])
    at(19.0, t_steps[2])
    at(19.5, m_steps[3])
    at(21.0, m_steps[4])
    at(24.0, m_steps[5])
    at(25.0, routing_rows)
    at(30.0, routing_ahead)
    at(40.0, routing_turn)
    at(55.0, t_steps[3])
    at(72.0, t_steps[4])
    at(77.0, t_steps[5])
    blocks = width // col
    for r in range(2):
        for s in range(0, blocks, 2):
            at(78.0 + 8.0 * r + s, pack, r, s, min(s + 2, blocks))
    ready = 94.0
    for e in range(2):
        when = max(ready, done[2 * e + 1])
        at(when, z_done, 2 * e)
        at(when, z_done, 2 * e + 1)
        for n in range(ff // fcol):
            at(when + 0.1 + n * 1.5, hidden, e, n)
        ready = when + 5.0
    at(ready, settle_tokens)
    for q in range(PARTS):
        when = max(done[4 + q], ready + (10.0 if q else 0.1))
        at(when, z_done, 4 + q)
        at(when + 0.01, down, q)
        at(when + 1.0, give, q)
        at(when + 5.0, y_first, q)
        at(when + 10.0, y_second, q)
        at(when + 19.0, y_third, q)
        at(when + 22.0, x_second, q)
        at(when + 25.0, x_third, q)
        ready = when
    for _, _, f, a in sorted(plan, key=lambda item: item[:2]):
        f(*a)
    for copy in sent + back_log:
        copy.wait_send()


def shards(nz, tokens, tokens_dot, router, router_dot, expert_ids, priority, w_gate, w_up, w_down):
    nx, ny, nc = GRID
    td, width = tokens.shape
    units = w_gate.shape[1]
    ff = units * nz
    dq = width // PARTS
    qw = 2 * dq
    hops = max(nz // 2, 1)
    pieces = 4 + PARTS
    vmem = pl.BlockSpec(memory_space=pltpu.VMEM)
    hbm = pl.BlockSpec(memory_space=pl.ANY)
    dma = pltpu.SemaphoreType.DMA
    shape = jax.ShapeDtypeStruct((td, width), BF16)
    group = nc * nx * td
    scratch = [
        pltpu.VMEM((2, ff, width), BF16),
        pltpu.VMEM((2, ff, width), BF16),
        pltpu.VMEM((PARTS, 2, ff, dq), BF16),
        pltpu.VMEM((ny, nc, nx, td, 2 * width), BF16),
        pltpu.VMEM((ny, nc, nx, td, 4 * LANES), F32),
        pltpu.VMEM((2, 2, CAP, width), BF16),
        pltpu.VMEM((2, 2, CAP, ff), BF16),
        pltpu.VMEM((2 * CAP, ny * group), BF16),
        pltpu.VMEM((ny, nc, nx * td, 2 * CAP), BF16),
        pltpu.VMEM((2, 2, CAP, 1), F32),
        pltpu.VMEM((2 * CAP, qw), BF16),
        pltpu.VMEM((2, ny, nx, td, qw), F32),
        pltpu.VMEM((2, nx, td, qw), F32),
        pltpu.VMEM((ny, 8, group), F32),
        pltpu.VMEM((PARTS, ny, nx, td, qw), BF16),
        pltpu.VMEM((PARTS, nx, td, qw), BF16),
        pltpu.VMEM((PARTS, 2, nx, td, qw), BF16),
        pltpu.VMEM((PARTS, td, qw), BF16),
        pltpu.VMEM((PARTS, 2, td, qw), BF16),
        dma((pieces, 2, hops)), dma((pieces, 2, hops)),
        dma((12,)), dma((12,)), dma((12,)), dma((12,)),
        dma((PARTS, 4)), dma((PARTS, 4)), dma((PARTS, 4)), dma((PARTS, 4)), dma((PARTS, 4)), dma((PARTS, 4)),
        dma((pieces,)),
    ]
    return pl.pallas_call(
        functools.partial(body, nz),
        out_shape=(shape, shape),
        in_specs=[vmem] * 6 + [hbm] * 3,
        out_specs=(vmem, vmem),
        scratch_shapes=scratch,
        compiler_params=pltpu.CompilerParams(
            collective_id=0, has_side_effects=True, vmem_limit_bytes=VMEM_BYTES),
    )(tokens, tokens_dot, router, router_dot, expert_ids, priority.reshape(td, 1), w_gate, w_up, w_down)


def solution(mesh):
    return jax.shard_map(
        functools.partial(shards, mesh.shape["dp"]),
        mesh=mesh,
        in_specs=(
            P(("dp", "expert"), None),
            P(("dp", "expert"), None),
            P(),
            P(),
            P(("dp", "expert"), None),
            P(("dp", "expert")),
            P("expert", "dp", None),
            P("expert", "dp", None),
            P("expert", "dp", None),
        ),
        out_specs=(P(("dp", "expert"), None), P(("dp", "expert"), None)),
        check_vma=False,
    )
```

time: 420 us -> 280 us (0.67)
  Pallas kernels: 0 us -> 271 us
  waiting for transfers between devices: 204 us -> 0 us
  local copies, waits for them, and re-layouts: 101 us -> 7.41 us
  other arithmetic: 42.2 us -> 0 us
  matrix products: 30.7 us -> 0 us
  starting transfers between devices: 23.3 us -> 0 us
  between operations: 14.2 us -> 0.66 us
    pallas_call x0 -> x1, Pallas kernels: none -> 271 us  [shards(): pl.pallas_call(functools.partial(body, nz), out_shape=(shape, shape), in_...]
    all_to_all x3 -> x0, waiting for transfers between devices: 173 us -> none  [the longest x1 86.7 us: shards(): lax.all_to_all(outgoing, 'expert', split_axis=0, concat_axis=0, tiled=True)]
    reshape x5 -> x1, local copies, waits for them, and re-layouts: 33.8 us -> 0.7 us  [shards(): priority.reshape(td, 1)]
    dot_general x8 -> x0, matrix products: 30.7 us -> none  [the longest x1 8.9 us: shards(): jnp.einsum('ecsm,semrd->ercd', placing, arrived, preferred_element_type=j...]
    gather x3 -> x0, other arithmetic: 30.2 us -> none  [the longest x1 30.2 us: shards(): priority[owner_tok]]
    all_gather x3 -> x0, waiting for transfers between devices: 28.7 us -> none  [the longest x1 28.7 us: shards(): down_piece = lax.all_gather(w_down, 'dp', axis=1, tiled=True)]
    gather x4 -> x0, local copies, waits for them, and re-layouts: 23.6 us -> none  [the longest x1 17.7 us: shards(): landed[target].reshape(tok_count, TOP, 2, feat_width).astype(jnp.float32)]
    all_to_all x3 -> x0, starting transfers between devices: 23.2 us -> none  [the longest x1 8.18 us: shards(): lax.all_to_all(out_ranks, 'expert', split_axis=0, concat_axis=0, tiled=True)]
  transfers between devices with their start and end apart: 6 -> 0, of which waited for: 3 -> 0; matrix products, arithmetic and copies ran while one was open for 23% -> 0% of each run, Pallas kernels for 0% -> 0%
where the time goes in v1:
time: 280 us; the launch traced here: 279 us
  Pallas kernels  271 us (97%)
  local copies, waits for them, and re-layouts  7.41 us (3%)
    pallas_call x1, Pallas kernels, shards(): pl.pallas_call(functools.partial(body, nz), out_shape=(shape, shape), in_...  271 us
    unnamed x11, local copies, waits for them, and re-layouts  6.71 us

profile of v1, /device:TPU:8, one launch (start us, length us, event | category | flops | bytes accessed | tf_op | source)
XLA Modules:
  0.0 278.7 jit_solution(7271214717862115777)
XLA Ops:
  0.6 0.0 copy-start.2
  0.6 1.4 copy.13.ids
  2.0 0.0 copy-done.2
  2.0 0.7 copy.14.rank
  2.7 0.0 copy-start
  2.7 2.0 copy.11.rout
  4.7 0.0 copy-done
  4.7 1.0 copy.12.routd
  5.7 270.6 %shard_map.104 = (bf16[48,2048]{1,0:T(8,128)(2,1)}, bf16[48,2048]{1,0:T(8,128)(2,1)}) custom-call(bf16[48,2048]{1,0:T(8,128)(2,1)} %tok.1, bf16[48,2048]{1,0:T(8,128)(2,1)} %tokd.1, bf16[2048,64]{1,0:T(8,128)(2,1)} %copy.11.rout, bf16[2048,64]{1,0:T(8,128)(2,1)} %copy.12.routd, s32[48,8]{1,0:T(8,128)} %copy.13.ids, s32[48,1]{1,0:T(8,128)} %copy.14.rank, ...), custom_call_target="tpu_custom_call" | custom-call | tf_op jit(solution)/shard_map/pallas_call | solution.py:490
  276.3 0.0 copy-start.1
  276.3 1.7 copy.17
  278.0 0.0 copy-done.1
  278.0 0.7 copy.18
Async XLA Ops:
  0.6 1.4 copy-start.2
  2.7 2.0 copy-start
  276.3 1.7 copy-start.1

commit v2 on v1

v2 whole, which is shorter than its diff:
```python
import functools

import jax
import jax.numpy as jnp
from jax import lax
from jax.experimental import pallas as pl
from jax.experimental.pallas import tpu as pltpu
from jax.sharding import PartitionSpec as P

GRID = (4, 4, 2)
CAP = 192
PARTS = 8
AHEAD = 2.0
DEEP = 4
LANES = 64
VMEM_BYTES = 66_500_000
F32 = jnp.float32
BF16 = jnp.bfloat16


def ring_order(first, pieces, hops, cost, latency):
    order = [(p, h) for h in range(1, hops) for p in range(first)]
    last = [(p, hops) for p in range(first)]
    for k in range(pieces - first + hops - 1):
        if k < hops - 1:
            order += last[k::hops - 1]
        order += [(first + k - h + 1, h) for h in range(1, hops + 1) if first <= first + k - h + 1 < pieces]
    clock, landed, timed = 0.0, {}, []
    for p, h in order:
        clock = max(clock, landed.get((p, h - 1), 0.0))
        timed.append((clock, p, h))
        clock += cost[p] * (0.5 if h == hops else 1.0)
        landed[p, h] = clock + latency
    return timed, {p: landed[p, hops] for p in range(pieces)}


def body(nz, tok, tokd, rout, routd, ids, rank, wg, wu, wd, out, outd,
         g_all, u_all, d_all, t_all, m_all, x_all, hid, place, place_t, slot_g, yy, keep, xsum, rows,
         c_in, a_in2, a_in1, b_in2, b_in1,
         zs, zr, ts, tr, ms, mr, cs, cr, rs, rr, loc):
    nx, ny, nc = GRID
    me = lax.axis_index("expert")
    z = lax.axis_index("dp")
    c = lax.rem(me, nc)
    y = lax.rem(lax.div(me, nc), ny)
    x = lax.div(me, nc * ny)
    td, width = tok.shape
    units = wg.shape[1]
    ff = units * nz
    dq = width // PARTS
    qw = 2 * dq
    top = ids.shape[0]
    hops = nz // 2

    def dev(zz, xx, yc, cc):
        return {"dp": zz, "expert": (xx * ny + yc) * nc + cc}

    def step(v, by, n):
        return lax.rem(v + (by + n), n)

    z_nb = [dev(step(z, s, nz), x, y, c) for s in (1, -1)]
    x_nb = [dev(z, step(x, s, nx), y, c) for s in (1, -1)]
    y_nb = [dev(z, x, step(y, s, ny), c) for s in (1, -1)]
    sib = dev(z, x, y, 1 - c)

    partners = [sib] + (z_nb if nz > 1 else []) + (x_nb if nx > 1 else []) + (y_nb if ny > 1 else [])
    barrier = pltpu.get_barrier_semaphore()
    for p in partners:
        pl.semaphore_signal(barrier, inc=1, device_id=p, device_id_type=pl.DeviceIdType.MESH)
    pl.semaphore_wait(barrier, len(partners))

    sent = []

    def send(src, dst, ssem, rsem, device):
        copy = pltpu.make_async_remote_copy(
            src_ref=src, dst_ref=dst, send_sem=ssem, recv_sem=rsem,
            device_id=device, device_id_type=pl.DeviceIdType.MESH)
        copy.start()
        return copy

    def arrived(dst, ssem, rsem, device):
        pltpu.make_async_remote_copy(
            src_ref=dst, dst_ref=dst, send_sem=ssem, recv_sem=rsem,
            device_id=device, device_id_type=pl.DeviceIdType.MESH).wait_recv()

    half_units = units // 2

    def piece_own(p):
        if p < 4:
            return (wg, wu)[p % 2].at[p // 2]
        return wd.at[:, :, pl.ds((p - 4) * dq, dq)]

    def piece_view(p, zz):
        at = pl.ds(pl.multiple_of(zz * units, units), units)
        if p < 4:
            return (g_all, u_all)[p % 2].at[p // 2, at]
        return d_all.at[p - 4, :, at]

    def piece_half(p, zz, d):
        if p < 4:
            at = pl.ds(pl.multiple_of(zz * units + d * half_units, half_units), half_units)
            return (g_all, u_all)[p % 2].at[p // 2, at]
        return d_all.at[p - 4, d, pl.ds(pl.multiple_of(zz * units, units), units)]

    pieces = 4 + PARTS

    def own_copy(p):
        return pltpu.make_async_copy(piece_own(p), piece_view(p, z), loc.at[p])

    def z_send(p, h):
        for d in range(2):
            sign = (-1, 1)[d]
            if h == 1:
                src, dst = piece_own(p), piece_view(p, z)
            else:
                origin = step(z, sign * (h - 1), nz)
                arrived(piece_view(p, origin), zs.at[p, d, h - 2], zr.at[p, d, h - 2], z_nb[d])
                src = piece_view(p, origin) if h < hops else piece_half(p, origin, d)
                dst = src
            sent.append(send(src, dst, zs.at[p, d, h - 1], zr.at[p, d, h - 1], z_nb[d]))

    def z_done(p):
        own_copy(p).wait()
        if nz > 1:
            for d in range(2):
                origin = step(z, (-1, 1)[d] * hops, nz)
                arrived(piece_half(p, origin, d), zs.at[p, d, hops - 1], zr.at[p, d, hops - 1], z_nb[d])

    nt = (((1,), (1,)), ((), ()))

    def gather_steps(buf, ssem, rsem, log, lo, size, y_leads):
        cols = pl.ds(lo, size)
        pos1, n1, nb1, pos2, n2, nb2 = (y, ny, y_nb, x, nx, x_nb) if y_leads else (x, nx, x_nb, y, ny, y_nb)

        def part(d):
            return cols if d is None else pl.ds(lo + d * (size // 2), size // 2)

        def view1(i, d=None):
            return buf.at[i, c, x, :, part(d)] if y_leads else buf.at[y, c, i, :, part(d)]

        def view2(i, d=None, core=c):
            return buf.at[:, core, i, :, part(d)] if y_leads else buf.at[i, core, :, :, part(d)]

        def one(base, view, pos, nb):
            for d in range(2):
                log.append(send(view(pos), view(pos), ssem.at[base + d], rsem.at[base + d], nb[d]))

        def two(base, view, pos, n, nb):
            for d in range(2):
                origin = step(pos, (-1, 1)[d], n)
                arrived(view(origin), ssem.at[base + d], rsem.at[base + d], nb[d])
                log.append(send(view(origin, d), view(origin, d), ssem.at[base + 2 + d], rsem.at[base + 2 + d], nb[d]))

        def three(base, view, pos, n, nb):
            for d in range(2):
                arrived(view(step(pos, (-2, 2)[d], n), d), ssem.at[base + 2 + d], rsem.at[base + 2 + d], nb[d])

        def cross(k):
            i = step(pos2, (0, -1, 1, 2)[k], n2)
            log.append(send(view2(i), view2(i), ssem.at[8 + k], rsem.at[8 + k], sib))

        def first_start():
            if n1 > 1:
                one(0, view1, pos1, nb1)

        def first_relay():
            if n1 > 1:
                two(0, view1, pos1, n1, nb1)

        def second_start():
            if n1 > 1:
                three(0, view1, pos1, n1, nb1)
            if n2 > 1:
                one(4, view2, pos2, nb2)
            cross(0)

        def second_relay():
            if n2 > 1:
                two(4, view2, pos2, n2, nb2)
                cross(1)
                cross(2)

        def second_end():
            if n2 > 1:
                three(4, view2, pos2, n2, nb2)
                cross(3)

        def end():
            for k in range(4 if n2 > 1 else 1):
                i = step(pos2, (0, -1, 1, 2)[k], n2)
                arrived(view2(i, None, 1 - c), ssem.at[8 + k], rsem.at[8 + k], sib)

        return first_start, first_relay, second_start, second_relay, second_end, end

    t_log, m_log = [], []
    t_steps = [gather_steps(t_all, ts.at[a], tr.at[a], t_log, a * width, width, a == 1) for a in range(2)]
    m_steps = gather_steps(m_all, ms, mr, m_log, 0, 4 * LANES, False)

    def tokens_step(k):
        for a in range(2):
            t_steps[a][k]()

    def tokens_start():
        t_all[y, c, x, :, pl.ds(0, width)] = tok[...]
        t_all[y, c, x, :, pl.ds(width, width)] = tokd[...]
        tokens_step(0)

    def routing_start():
        logits = lax.dot_general(tok[...], rout[...], nt, preferred_element_type=F32)
        logits_dot = lax.dot_general(tokd[...], rout[...], nt, preferred_element_type=F32) + lax.dot_general(
            tok[...], routd[...], nt, preferred_element_type=F32)
        high = lax.div(rank[...], 128)
        low = rank[...] - 128 * high
        lines = [ids[...].astype(F32), high.astype(F32), low.astype(F32), jnp.zeros((14 - top, td), F32)]
        lines = jnp.concatenate(lines, axis=0).astype(BF16)
        eye = lax.broadcasted_iota(jnp.int32, (td, td), 0) == lax.broadcasted_iota(jnp.int32, (td, td), 1)
        turned = lax.dot_general(jnp.where(eye, 1.0, 0.0).astype(BF16), lines, nt, preferred_element_type=F32)
        lane = lax.broadcasted_iota(jnp.int32, (td, LANES), 1).astype(F32)
        member = jnp.zeros((td, LANES), F32)
        for k in range(top):
            member = jnp.where(lane == turned[:, k:k + 1], 1.0, member)
        chosen = member > 0.5
        expo = jnp.where(chosen, jnp.exp(jnp.where(chosen, logits, 0.0)), 0.0)
        gates = expo / jnp.sum(expo, axis=1, keepdims=True)
        sel_dot = jnp.where(chosen, logits_dot, 0.0)
        gates_dot = jnp.where(chosen, gates * (sel_dot - jnp.sum(gates * sel_dot, axis=1, keepdims=True)), 0.0)
        own_rank = jnp.broadcast_to(turned[:, top:top + 1] * 128.0 + turned[:, top + 1:top + 2], (td, LANES))
        m_all[y, c, x] = jnp.concatenate([gates, gates_dot, member, own_rank], axis=1)
        m_steps[0]()

    group = nc * nx * td
    slots = 2 * CAP

    def routing_rows():
        lane = lax.broadcasted_iota(jnp.int32, (group, 4 * LANES), 1)
        lane_s = lax.broadcasted_iota(jnp.int32, (group, 128), 1)

        @pl.loop(0, ny)
        def _(i):
            m = m_all[i].reshape(group, 4 * LANES)
            picked = jnp.zeros((group, 128), F32)
            columns = [3 * LANES] + [2 * LANES + 2 * me + e for e in range(2)]
            columns += [2 * me + e for e in range(2)] + [LANES + 2 * me + e for e in range(2)]
            for j, col in enumerate(columns):
                v = jnp.sum(jnp.where(lane == col, m, 0.0), axis=1, keepdims=True)
                picked = jnp.where(lane_s == j, v, picked)
            rows[i] = jnp.transpose(picked)[0:8]

    def routing_ahead():
        whole = jnp.concatenate([rows[i] for i in range(ny)], axis=1)
        rank_t = whole[0:1]
        ahead = jnp.zeros((8, ny * group), F32)
        for i in range(ny):
            rank_s = m_all[i].reshape(group, 4 * LANES)[:, 3 * LANES:3 * LANES + 1]
            lower = jnp.where(rank_s < rank_t, 1.0, 0.0).astype(BF16)
            ahead = ahead + jnp.dot(rows[i].astype(BF16), lower, preferred_element_type=F32)
        seat = lax.broadcasted_iota(jnp.int32, (CAP, ny * group), 0).astype(F32)
        for e in range(2):
            here = jnp.where(whole[1 + e:2 + e] > 0.5, ahead[1 + e:2 + e], -1.0)
            hit = here == seat
            place[pl.ds(e * CAP, CAP)] = jnp.where(hit, 1.0, 0.0).astype(BF16)
            for r in range(2):
                slot_g[r, e] = jnp.sum(jnp.where(hit, whole[3 + 2 * r + e:4 + 2 * r + e], 0.0), axis=1, keepdims=True)

    def routing_turn():
        for i in range(ny):
            block = place[:, pl.ds(i * group, group)].astype(F32)
            place_t[i] = jnp.transpose(block).astype(BF16).reshape(nc, nx * td, slots)

    col = min(256, width)

    def pack(r, lo, hi):
        @pl.loop(lo, hi)
        def _(n):
            at = pl.multiple_of(n * col, col)
            picked = t_all[:, :, :, :, pl.ds(pl.multiple_of(r * width + at, col), col)].reshape(ny * group, col)
            res = jnp.dot(place[...], picked, preferred_element_type=F32).astype(BF16)
            for e in range(2):
                x_all[e, r, :, pl.ds(at, col)] = res[e * CAP:(e + 1) * CAP]

    fcol = 256 if ff % 256 == 0 else ff
    def hidden(e, n):
        at = pl.ds(n * fcol, fcol)
        both = x_all[e].reshape(slots, width)
        ga = lax.dot_general(both, g_all[e, at], nt, preferred_element_type=F32)
        ua = lax.dot_general(both, u_all[e, at], nt, preferred_element_type=F32)
        gp, gt, up, ut = ga[:CAP], ga[CAP:], ua[:CAP], ua[CAP:]
        sigma = 1.0 / (1.0 + jnp.exp(-gp))
        hid[e, 0, :, at] = (gp * sigma * up).astype(BF16)
        hid[e, 1, :, at] = (sigma * (1.0 + gp * (1.0 - sigma)) * gt * up + gp * sigma * ut).astype(BF16)

    back_log = []

    def down(q):
        for e in range(2):
            res = jnp.dot(hid[e].reshape(slots, ff), d_all[q, e], preferred_element_type=F32)
            prim, tang = res[:CAP], res[CAP:]
            g, gd = slot_g[0, e], slot_g[1, e]
            yy[pl.ds(e * CAP, CAP), pl.ds(0, dq)] = (g * prim).astype(BF16)
            yy[pl.ds(e * CAP, CAP), pl.ds(dq, dq)] = (gd * prim + g * tang).astype(BF16)

    y_turn = (2, 1, -1, 0) if ny > 1 else (0,)

    def give(q):
        cols = pl.ds(q * qw, qw)
        for k, by in enumerate(y_turn):
            i = step(y, by, ny)
            res = jnp.dot(place_t[i, 1 - c], yy[...], preferred_element_type=F32)
            t_all[i, 0, :, :, cols] = res.astype(BF16).reshape(nx, td, qw)
            back_log.append(send(t_all.at[i, 0, :, :, cols], c_in.at[q, i], cs.at[q, k], cr.at[q, k], sib))
        for by in y_turn:
            i = step(y, by, ny)
            res = jnp.dot(place_t[i, c], yy[...], preferred_element_type=F32)
            keep[q % DEEP, i] = res.reshape(nx, td, qw)

    def spot(a, k):
        return (y, x)[a ^ k], (ny, nx)[a ^ k], (y_nb, x_nb)[a ^ k]

    def meet(q):
        for k, by in enumerate(y_turn):
            i = step(y, by, ny)
            arrived(c_in.at[q, i], cs.at[q, k], cr.at[q, k], sib)
            keep[q % DEEP, i] = keep[q % DEEP, i] + c_in[q, i].astype(F32)

    hw = dq // 2

    def block(q, a, i):
        cols = pl.ds(a * dq, dq)
        return keep[q % DEEP, i, :, :, cols] if a == 0 else keep[q % DEEP, :, i, :, cols]

    def relay_out(v, stage, into, base, q, a, nb):
        stage[...] = v.astype(BF16)
        for d in range(2):
            at = (slice(None),) * (len(into.shape) - 1) + (pl.ds(d * hw, hw),)
            back_log.append(send(stage.at[at], into.at[at], rs.at[q, a, base + d], rr.at[q, a, base + d], nb[d]))

    def relay_on(v, stage, into2, into1, base, q, a, d, nb):
        at = (slice(None),) * (len(into2.shape) - 1) + (pl.ds(d * hw, hw),)
        got = into2.at[at]
        arrived(got, rs.at[q, a, base + d], rr.at[q, a, base + d], nb)
        halves = [v[..., :hw], v[..., hw:]]
        halves[d] = halves[d] + got[...].astype(F32)
        stage[...] = jnp.concatenate(halves, axis=-1).astype(BF16)
        back_log.append(send(stage, into1, rs.at[q, a, base + 2 + d], rr.at[q, a, base + 2 + d], nb))

    def relay_end(v, into1, base, q, a, nb):
        for d in range(2):
            arrived(into1.at[d], rs.at[q, a, base + 2 + d], rr.at[q, a, base + 2 + d], nb[d])
            v = v + into1[d].astype(F32)
        return v

    def stage(q, a, k):
        return t_all.at[k, 1, :, :, pl.ds(q * qw + a * dq, dq)]

    def stage2(q, a, k):
        return t_all.at[ny - 1, 1, k, :, pl.ds(q * qw + a * dq, dq)]

    def back_first(q):
        meet(q)
        for a in range(2):
            pos, n, nb = spot(a, 0)
            if n > 1:
                relay_out(block(q, a, step(pos, 2, n)), stage(q, a, 0), a_in2.at[q, a], 0, q, a, nb)

    def back_second(q):
        for a in range(2):
            pos, n, nb = spot(a, 0)
            if n > 1:
                for d in range(2):
                    relay_on(block(q, a, step(pos, (1, -1)[d], n)), stage(q, a, 1 + d), a_in2.at[q, a],
                             a_in1.at[q, a, d], 0, q, a, d, nb[d])

    def back_third(q):
        for a in range(2):
            pos, n, nb = spot(a, 0)
            v = block(q, a, pos)
            if n > 1:
                v = relay_end(v, a_in1.at[q, a], 0, q, a, nb)
            xsum[q % DEEP, a] = v
            pos, n, nb = spot(a, 1)
            if n > 1:
                relay_out(xsum[q % DEEP, a, step(pos, 2, n)], stage2(q, a, 0), b_in2.at[q, a], 4, q, a, nb)

    def back_fourth(q):
        for a in range(2):
            pos, n, nb = spot(a, 1)
            if n > 1:
                for d in range(2):
                    relay_on(xsum[q % DEEP, a, step(pos, (1, -1)[d], n)], stage2(q, a, 1 + d), b_in2.at[q, a],
                             b_in1.at[q, a, d], 4, q, a, d, nb[d])

    def back_fifth(q):
        for a in range(2):
            pos, n, nb = spot(a, 1)
            v = xsum[q % DEEP, a, pos]
            if n > 1:
                v = relay_end(v, b_in1.at[q, a], 4, q, a, nb)
            (out, outd)[a][:, pl.ds(q * dq, dq)] = v.astype(BF16)

    def settle_tokens():
        for copy in t_log + m_log:
            copy.wait_send()

    plan = []

    def at(t, f, *a):
        plan.append((t, len(plan), f, a))

    tau = 8.8
    cost = [tau] * 4 + [2 * tau / PARTS] * PARTS
    if nz > 1:
        order, done = ring_order(4, pieces, hops, cost, 2.0)
    else:
        order, done = [], {p: 60.0 + 8.0 * p for p in range(pieces)}
    for t, p, h in order:
        at(t - AHEAD - (5.0 if h == 1 and p >= 4 else 0.0), z_send, p, h)
    for p in range(pieces):
        at(0.1, lambda p: own_copy(p).start(), p)
    at(0.2, routing_start)
    at(0.3, tokens_start)
    for t, k in ((6.0, 1), (9.0, 2), (13.0, 3), (15.0, 4), (17.0, 5)):
        at(t, m_steps[k])
    for t, k in ((9.5, 1), (13.5, 2), (34.0, 3), (44.0, 4), (48.0, 5)):
        at(t, tokens_step, k)
    at(18.0, routing_rows)
    at(22.0, routing_ahead)
    at(28.0, routing_turn)
    blocks = width // col
    for r in range(2):
        for s in range(0, blocks, 2):
            at(49.0 + 4.0 * r + s, pack, r, s, min(s + 2, blocks))
    ready = 60.0
    for e in range(2):
        when = max(ready, done[2 * e], done[2 * e + 1])
        at(when, z_done, 2 * e)
        at(when, z_done, 2 * e + 1)
        for n in range(ff // fcol):
            at(when + 0.1 + n * 1.5, hidden, e, n)
        ready = when + 5.0
    at(ready, settle_tokens)
    turn = []
    for q in range(PARTS):
        turn.append(max(done[4 + q], ready + (3.0 if q else 0.1)))
        ready = turn[-1]
    for q in range(PARTS):
        at(turn[q], z_done, 4 + q)
        at(turn[q] + 0.1, down, q)
        at(turn[q] + 0.2, give, q)
        for f, later in ((back_first, 3.5), (back_second, 7.0), (back_third, 11.5), (back_fourth, 14.5), (back_fifth, 17.5)):
            at(turn[q] + later, f, q)
    for _, _, f, a in sorted(plan, key=lambda item: item[:2]):
        f(*a)
    for copy in sent + back_log:
        copy.wait_send()


def shards(nz, tokens, tokens_dot, router, router_dot, expert_ids, priority, w_gate, w_up, w_down):
    nx, ny, nc = GRID
    td, width = tokens.shape
    units = w_gate.shape[1]
    ff = units * nz
    dq = width // PARTS
    qw = 2 * dq
    hops = max(nz // 2, 1)
    pieces = 4 + PARTS
    vmem = pl.BlockSpec(memory_space=pltpu.VMEM)
    hbm = pl.BlockSpec(memory_space=pl.ANY)
    dma = pltpu.SemaphoreType.DMA
    shape = jax.ShapeDtypeStruct((td, width), BF16)
    group = nc * nx * td
    scratch = [
        pltpu.VMEM((2, ff, width), BF16),
        pltpu.VMEM((2, ff, width), BF16),
        pltpu.VMEM((PARTS, 2, ff, dq), BF16),
        pltpu.VMEM((ny, nc, nx, td, 2 * width), BF16),
        pltpu.VMEM((ny, nc, nx, td, 4 * LANES), F32),
        pltpu.VMEM((2, 2, CAP, width), BF16),
        pltpu.VMEM((2, 2, CAP, ff), BF16),
        pltpu.VMEM((2 * CAP, ny * group), BF16),
        pltpu.VMEM((ny, nc, nx * td, 2 * CAP), BF16),
        pltpu.VMEM((2, 2, CAP, 1), F32),
        pltpu.VMEM((2 * CAP, qw), BF16),
        pltpu.VMEM((DEEP, ny, nx, td, qw), F32),
        pltpu.VMEM((DEEP, 2, nx, td, dq), F32),
        pltpu.VMEM((ny, 8, group), F32),
        pltpu.VMEM((PARTS, ny, nx, td, qw), BF16),
        pltpu.VMEM((PARTS, 2, 4, td, dq), BF16),
        pltpu.VMEM((PARTS, 2, 2, 4, td, dq), BF16),
        pltpu.VMEM((PARTS, 2, td, dq), BF16),
        pltpu.VMEM((PARTS, 2, 2, td, dq), BF16),
        dma((pieces, 2, hops)), dma((pieces, 2, hops)),
        dma((2, 12)), dma((2, 12)), dma((12,)), dma((12,)),
        dma((PARTS, 4)), dma((PARTS, 4)), dma((PARTS, 2, 8)), dma((PARTS, 2, 8)),
        dma((pieces,)),
    ]
    return pl.pallas_call(
        functools.partial(body, nz),
        out_shape=(shape, shape),
        in_specs=[vmem] * 6 + [hbm] * 3,
        out_specs=(vmem, vmem),
        scratch_shapes=scratch,
        compiler_params=pltpu.CompilerParams(
            collective_id=0, has_side_effects=True, vmem_limit_bytes=VMEM_BYTES),
    )(tokens, tokens_dot, router.T, router_dot.T, expert_ids.T, priority.reshape(1, td), w_gate, w_up, w_down)


def solution(mesh):
    return jax.shard_map(
        functools.partial(shards, mesh.shape["dp"]),
        mesh=mesh,
        in_specs=(
            P(("dp", "expert"), None),
            P(("dp", "expert"), None),
            P(),
            P(),
            P(("dp", "expert"), None),
            P(("dp", "expert")),
            P("expert", "dp", None),
            P("expert", "dp", None),
            P("expert", "dp", None),
        ),
        out_specs=(P(("dp", "expert"), None), P(("dp", "expert"), None)),
        check_vma=False,
    )
```

time: 280 us -> 231 us (0.82)
  Pallas kernels: 271 us -> 228 us
  local copies, waits for them, and re-layouts: 7.41 us -> 2.34 us
    pallas_call x1, Pallas kernels: 271 us -> 228 us  [shards(): pl.pallas_call(functools.partial(body, nz), out_shape=(shape, shape), in_...]
    unnamed x11 -> x4, local copies, waits for them, and re-layouts: 6.71 us -> 2.34 us
where the time goes in v2:
time: 231 us
  Pallas kernels  228 us (99%)
  local copies, waits for them, and re-layouts  2.34 us (1%)
    pallas_call x1, Pallas kernels, shards(): pl.pallas_call(functools.partial(body, nz), out_shape=(shape, shape), in_...  228 us

profile of v2, /device:TPU:8, one launch (start us, length us, event | category | flops | bytes accessed | tf_op | source)
XLA Modules:
  0.0 230.7 jit_solution(1430034206723465343)
XLA Ops:
  0.6 227.7 %shard_map.104 = (bf16[48,2048]{1,0:T(8,128)(2,1)}, bf16[48,2048]{1,0:T(8,128)(2,1)}) custom-call(bf16[48,2048]{1,0:T(8,128)(2,1)} %tok.1, bf16[48,2048]{1,0:T(8,128)(2,1)} %tokd.1, bf16[64,2048]{1,0:T(8,128)(2,1)} %bitcast.4, bf16[64,2048]{1,0:T(8,128)(2,1)} %bitcast.5, s32[8,48]{1,0:T(8,128)} %bitcast.6, s32[1,48]{1,0:T(1,128)} %bitcast.7, ...), custom_call_target="tpu_custom_call" | custom-call | tf_op jit(solution)/shard_map/pallas_call | solution.py:496
  228.4 0.0 copy-start
  228.4 1.7 copy.13
  230.0 0.0 copy-done
  230.0 0.7 copy.14
Async XLA Ops:
  228.4 1.7 copy-start

commit v3 on v2

--- a/solution.py
+++ b/solution.py
@@ -25,6 +25,12 @@
         if k < hops - 1:
             order += last[k::hops - 1]
         order += [(first + k - h + 1, h) for h in range(1, hops + 1) if first <= first + k - h + 1 < pieces]
+    if first == 4 and hops == 4 and pieces > 8:
+        order = [(p, 1) for p in range(4)] + [(0, 2), (1, 2), (4, 1), (2, 2), (3, 2)]
+        order += [(0, 3), (1, 3), (4, 2), (2, 3), (5, 1), (3, 3), (0, 4), (4, 3), (1, 4), (2, 4), (5, 2), (3, 4)]
+        order += [(4, 4), (6, 1), (5, 3), (6, 2), (5, 4), (7, 1)]
+        for k in range(6, pieces):
+            order += [(p, h) for p, h in ((k, 3), (k + 1, 2), (k + 2, 1), (k, 4)) if p < pieces]
     clock, landed, timed = 0.0, {}, []
     for p, h in order:
         clock = max(clock, landed.get((p, h - 1), 0.0))
@@ -440,13 +446,13 @@
     at(ready, settle_tokens)
     turn = []
     for q in range(PARTS):
-        turn.append(max(done[4 + q], ready + (3.0 if q else 0.1)))
+        turn.append(max(done[4 + q], ready + (4.5 if q else 0.1)))
         ready = turn[-1]
     for q in range(PARTS):
         at(turn[q], z_done, 4 + q)
         at(turn[q] + 0.1, down, q)
         at(turn[q] + 0.2, give, q)
-        for f, later in ((back_first, 3.5), (back_second, 7.0), (back_third, 11.5), (back_fourth, 14.5), (back_fifth, 17.5)):
+        for f, later in ((back_first, 5.0), (back_second, 10.0), (back_third, 16.0), (back_fourth, 21.0), (back_fifth, 26.0)):
             at(turn[q] + later, f, q)
     for _, _, f, a in sorted(plan, key=lambda item: item[:2]):
         f(*a)

time: 231 us -> 223 us (0.965)
  Pallas kernels: 228 us -> 220 us
    pallas_call x1, Pallas kernels: 228 us -> 220 us  [shards(): pl.pallas_call(functools.partial(body, nz), out_shape=(shape, shape), in_...]
where the time goes in v3:
time: 223 us
  Pallas kernels  220 us (99%)
  local copies, waits for them, and re-layouts  2.34 us (1%)
    pallas_call x1, Pallas kernels, shards(): pl.pallas_call(functools.partial(body, nz), out_shape=(shape, shape), in_...  220 us

profile of v3, /device:TPU:8, one launch (start us, length us, event | category | flops | bytes accessed | tf_op | source)
XLA Modules:
  0.0 223.0 jit_solution(16872265650713874230)
XLA Ops:
  0.6 220.0 %shard_map.104 = (bf16[48,2048]{1,0:T(8,128)(2,1)}, bf16[48,2048]{1,0:T(8,128)(2,1)}) custom-call(bf16[48,2048]{1,0:T(8,128)(2,1)} %tok.1, bf16[48,2048]{1,0:T(8,128)(2,1)} %tokd.1, bf16[64,2048]{1,0:T(8,128)(2,1)} %bitcast.4, bf16[64,2048]{1,0:T(8,128)(2,1)} %bitcast.5, s32[8,48]{1,0:T(8,128)} %bitcast.6, s32[1,48]{1,0:T(1,128)} %bitcast.7, ...), custom_call_target="tpu_custom_call" | custom-call | tf_op jit(solution)/shard_map/pallas_call | solution.py:502
  220.6 0.0 copy-start
  220.6 1.7 copy.13
  222.3 0.0 copy-done
  222.3 0.7 copy.14
Async XLA Ops:
  220.6 1.7 copy-start
